TPU v7x, 512 devices: a whole 4x4x16 slice. The times are simulated.
512 devices in a mesh: row: 32 (over y, x, core), col: 16 (over z).
Axes of the slice: x: 4, y: 4, z: 16, core: 2. Of those that a mesh axis runs over, the one named last changes fastest.
Arguments:
- vertex: float32 [8192, 8192], P('row', 'col'), may hold values from -0.046875 to 0.046875
- bubbles: float32 [4, 8192, 8192], P(None, 'row', 'col'), may hold values from 0.5 to 1.5
- site_panel: float32 [8192, 256], P('row', 'col'), may hold values from -6 to 6
- bond_sites: int32 [24576, 2], replicated, may hold values from 0 to 8191
- bond_class: int32 [24576], replicated, may hold values from 0 to 15
- coupling: float32 [16], replicated, may hold values from -4 to 4
Outputs:
- first_term: float32 [8192, 256], P('col', 'row')
- second_term: float32 [8192, 256], P('row', 'col')
- third_term: float32 [8192, 256], P('col', 'row')
- fourth_term: float32 [8192, 256], P('row', 'col')
All inputs are finite; a program needn't handle non-finite values.
Results may differ from a plain program's by a relative error of at most 0.0001.
Values sent between devices are 32-bit elements; how exact they have to be, the bound alone decides.
No kernel may reach another device: no remote copies, remote signals or barrier semaphores. Data moves between devices by JAX's collectives and lax.ppermute only.
A program may use at most 64 MiB of HBM per device.

v0:
```python
import jax
import jax.numpy as jnp
from jax import lax
from jax.sharding import PartitionSpec as P

HIGHEST = lax.Precision.HIGHEST


def transposed(weighted, piece):
    return lax.dot_general(
        weighted,
        piece,
        (((0,), (0,)), ((), ())),
        precision=HIGHEST,
        preferred_element_type=jnp.float32,
    )


def straight(weighted, piece):
    return jnp.dot(weighted, piece, precision=HIGHEST, preferred_element_type=jnp.float32)


def per_device(vertex, bubbles, site_panel, bond_sites, bond_class, coupling):
    rows_blk, cols_blk = vertex.shape
    row_start = lax.axis_index("row") * rows_blk
    col_start = lax.axis_index("col") * cols_blk
    classes = jnp.arange(coupling.shape[0], dtype=jnp.int32)
    strength = jnp.sum(
        jnp.where(bond_class[:, None] == classes[None, :], coupling[None, :], 0.0), axis=1
    )

    def place(block, first_site, second_site):
        local_row = first_site - row_start
        local_col = second_site - col_start
        inside = (
            (local_row >= 0) & (local_row < rows_blk) & (local_col >= 0) & (local_col < cols_blk)
        )
        local_row = jnp.where(inside, local_row, rows_blk)
        local_col = jnp.where(inside, local_col, cols_blk)
        return block.at[local_row, local_col].add(jnp.where(inside, strength, 0.0), mode="drop")

    full = place(vertex, bond_sites[:, 0], bond_sites[:, 1])
    full = place(full, bond_sites[:, 1], bond_sites[:, 0])
    weighted = [bubbles[step] * full for step in range(bubbles.shape[0])]
    results = []
    current = site_panel
    for couple in range(2):
        partial_value = transposed(
            weighted[2 * couple], lax.all_gather(current, "col", axis=1, tiled=True)
        )
        odd_term = lax.psum_scatter(partial_value, "row", scatter_dimension=1, tiled=True)
        partial_value = straight(
            weighted[2 * couple + 1], lax.all_gather(odd_term, "row", axis=1, tiled=True)
        )
        current = lax.psum_scatter(partial_value, "col", scatter_dimension=1, tiled=True)
        results += [odd_term, current]
    return (results[0], results[1], results[2], results[3])


def solution(mesh):
    in_specs = (P("row", "col"), P(None, "row", "col"), P("row", "col"), P(), P(), P())
    out_specs = (P("col", "row"), P("row", "col"), P("col", "row"), P("row", "col"))
    return jax.shard_map(
        per_device, mesh=mesh, in_specs=in_specs, out_specs=out_specs, check_vma=False
    )
```

profile of v0, /device:TPU:1, one launch (start us, length us, event | category | flops | bytes accessed | tf_op | source)
XLA Modules:
  0.0 724.4 jit_solution(16576725903242840462)
XLA Ops:
  7.2 2.2 fusion.9
  9.4 1.7 compare_select_fusion.3
  11.1 1.4 multiply_reduce_fusion
  12.5 1.5 and_reduce_fusion
  14.1 0.1 copy.10
  14.2 0.4 select_reduce_fusion
  14.7 131.6 %scatter_fusion = f32[131072]{0:T(1024)S(1)} fusion(f32[131072]{0:T(1024)S(1)} %bitcast.18, s32[24576]{0:T(1024)S(1)} %get-tuple-element.23, f32[24576]{0:T(1024)S(1)} %get-tuple-element.21), kind=kCustom, calls=%fused_computation | custom fusion | flops 24576 | bytes 393216
  146.4 131.6 %scatter_fusion.1 = f32[131072]{0:T(1024)S(1)} fusion(f32[131072]{0:T(1024)S(1)} %scatter_fusion, s32[24576]{0:T(1024)S(1)} %get-tuple-element.22, f32[24576]{0:T(1024)S(1)} %get-tuple-element.20), kind=kCustom, calls=%fused_computation.1 | custom fusion | flops 24576 | bytes 393216
  278.0 0.1 reshape.45
  278.1 30.5 %all_gather.12 = f32[256,256]{0,1:T(8,128)S(1)} all-gather(f32[256,16]{0,1:T(8,128)S(1)} %copy-done.3), channel_id=1, replica_groups=mesh['row'=32,'col'=16] {'col'}, dimensions={1}, use_global_device_ids=true | all-gather | bytes 278528 | tf_op jit(solution)/shard_map/all_gather | solution.py:49
  308.6 1.5 fusion.3
  310.1 0.0 reduce-scatter.7.cloned.1.call-start
  310.1 101.7 %reduce-scatter.5.cloned.1.call-done = f32[512,8]{0,1:T(8,128)} async-done(((f32[512,256]{0,1:T(8,128)}), f32[512,8]{0,1:T(8,128)}) %reduce-scatter.5.cloned.1.call-update) | async-done | bytes 16400 | tf_op jit(solution)/shard_map/reduce_scatter | solution.py:51
  411.8 26.2 %all_gather.13 = f32[512,256]{0,1:T(8,128)S(1)} all-gather(f32[512,8]{0,1:T(8,128)} %reduce-scatter.5.cloned.1.call-done), channel_id=1, replica_groups=mesh['row'=32,'col'=16] {'row'}, dimensions={1}, use_global_device_ids=true | all-gather | bytes 540672 | tf_op jit(solution)/shard_map/all_gather | solution.py:53
  438.0 1.3 fusion.2
  439.3 0.0 reduce-scatter.9.cloned.1.call-start
  439.4 55.7 %reduce-scatter.7.cloned.1.call-done = f32[256,16]{0,1:T(8,128)} async-done(((f32[256,256]{0,1:T(8,128)}), f32[256,16]{0,1:T(8,128)}) %reduce-scatter.7.cloned.1.call-update) | async-done | bytes 16400 | tf_op jit(solution)/shard_map/reduce_scatter | solution.py:55
  495.1 22.5 %all_gather.14 = f32[256,256]{0,1:T(8,128)S(1)} all-gather(f32[256,16]{0,1:T(8,128)} %reduce-scatter.7.cloned.1.call-done), channel_id=1, replica_groups=mesh['row'=32,'col'=16] {'col'}, dimensions={1}, use_global_device_ids=true | all-gather | bytes 278528 | tf_op jit(solution)/shard_map/all_gather | solution.py:49
  517.6 1.5 fusion.1
  519.1 0.0 reduce-scatter.11.cloned.1.call-start
  519.2 115.4 %reduce-scatter.9.cloned.1.call-done = f32[512,8]{0,1:T(8,128)} async-done(((f32[512,256]{0,1:T(8,128)}), f32[512,8]{0,1:T(8,128)}) %reduce-scatter.9.cloned.1.call-update) | async-done | bytes 16400 | tf_op jit(solution)/shard_map/reduce_scatter | solution.py:51
  634.6 26.2 %all_gather.15 = f32[512,256]{0,1:T(8,128)S(1)} all-gather(f32[512,8]{0,1:T(8,128)} %reduce-scatter.9.cloned.1.call-done), channel_id=1, replica_groups=mesh['row'=32,'col'=16] {'row'}, dimensions={1}, use_global_device_ids=true | all-gather | bytes 540672 | tf_op jit(solution)/shard_map/all_gather | solution.py:53
  660.8 1.3 fusion
  662.1 55.7 %reduce-scatter.11.cloned.1.call-done = f32[256,16]{0,1:T(8,128)} async-done(((f32[256,256]{0,1:T(8,128)}), f32[256,16]{0,1:T(8,128)}) %reduce-scatter.11.cloned.1.call-update) | async-done | bytes 16400 | tf_op jit(solution)/shard_map/reduce_scatter | solution.py:55
  (17 shorter events, 0.2 us)
Async XLA Ops:
  7.2 6.9 copy-start.1
  7.2 7.0 copy-start.2
  7.2 7.0 copy-start.4
  7.2 404.6 %reduce-scatter.5.cloned.1.call-start = ((), (), s32[]{:S(2)}) async-start(), calls=%async_computation.4 | async-start | bytes 540672 | tf_op jit(solution)/shard_map/reduce_scatter | solution.py:51
  146.3 131.8 %copy-start.3 = (f32[256,16]{0,1:T(8,128)S(1)}, f32[256,16]{0,1:T(8,128)}, u32[]{:S(2)}) copy-start(f32[256,16]{0,1:T(8,128)} %param.8) | copy-start | bytes 49156
  146.3 162.2 %copy-start = (f32[4,256,512]{2,1,0:T(8,128)S(1)}, f32[4,256,512]{2,1,0:T(8,128)}, u32[]{:S(2)}) copy-start(f32[4,256,512]{2,1,0:T(8,128)} %param.7) | copy-start | bytes 6291460
  310.1 185.0 %reduce-scatter.7.cloned.1.call-start = ((), (), s32[]{:S(2)}) async-start(), calls=%async_computation.5 | async-start | bytes 278528 | tf_op jit(solution)/shard_map/reduce_scatter | solution.py:55
  439.3 195.2 %reduce-scatter.9.cloned.1.call-start = ((), (), s32[]{:S(2)}) async-start(), calls=%async_computation.6 | async-start | bytes 540672 | tf_op jit(solution)/shard_map/reduce_scatter | solution.py:51
  519.1 198.7 %reduce-scatter.11.cloned.1.call-start = ((), (), s32[]{:S(2)}) async-start(), calls=%async_computation.7 | async-start | bytes 278528 | tf_op jit(solution)/shard_map/reduce_scatter | solution.py:55
Sparse Core Ops, SparseCore 0:
  310.2 101.5 reduce-scatter.4
  439.5 55.5 reduce-scatter.6
  519.2 115.2 reduce-scatter.8
  662.2 55.5 reduce-scatter.10
where the time goes:
time: 735 us; the launch traced here: 724 us
  waiting for transfers between devices  329 us (45%)
  other arithmetic  271 us (37%)
  blocking collectives  105 us (14%)
  between operations  13.9 us (2%)
    unnamed x5, other arithmetic  266 us
    reduce_scatter x2, waiting for transfers between devices, per_device(): lax.psum_scatter(partial_value, 'row', scatter_dimension=1, tiled=True)  217 us
    reduce_scatter x2, waiting for transfers between devices, per_device(): lax.psum_scatter(partial_value, 'col', scatter_dimension=1, tiled=True)  111 us
    all_gather x2, blocking collectives, per_device(): lax.all_gather(current, 'col', axis=1, tiled=True)  53 us
    all_gather x2, blocking collectives, per_device(): lax.all_gather(odd_term, 'row', axis=1, tiled=True)  52.4 us
  transfers between devices with their start and end apart: 4, of which 4 were waited for; matrix products, arithmetic and copies ran while one was open for 0% of the time, Pallas kernels for 0%

commit v1 on v0

v1 whole, which is shorter than its diff:
```python
import jax
import jax.numpy as jnp
from jax import lax
from jax.experimental import pallas as pl
from jax.experimental.pallas import tpu as pltpu
from jax.sharding import PartitionSpec as P

HIGHEST = lax.Precision.HIGHEST
LANES = 128
SLOTS = 8


def place_kernel(corner, coupling, sites, classes, vertex, full, rank, key, pull):
    rows, cols = vertex.shape
    groups = classes.shape[0]
    first = sites[pl.ds(0, groups, stride=2), :] if sites.ndim == 2 else sites[0]
    second = sites[pl.ds(1, groups, stride=2), :] if sites.ndim == 2 else sites[1]
    kind = classes[...]
    strength = jnp.zeros(kind.shape, jnp.float32)
    for index in range(coupling.shape[0]):
        strength = jnp.where(kind == index, coupling[index], strength)
    pull[...] = strength
    count = jnp.zeros((8, LANES), jnp.int32)
    for way, (end, start) in enumerate(((first, second), (second, first))):
        row = end - corner[0]
        col = start - corner[1]
        inside = (row >= 0) & (row < rows) & (col >= 0) & (col < cols)
        key[pl.ds(way * groups, groups), :] = row * cols + col
        hit = inside.astype(jnp.int32)
        for step in range(groups // 8):
            now = hit[8 * step : 8 * step + 8]
            rank[pl.ds(way * groups + 8 * step, 8), :] = jnp.where(now == 1, count, -(1 << 20))
            count = count + now
    before = jnp.zeros((1, LANES), jnp.int32)
    offsets = []
    for sub in range(8):
        offsets.append(before)
        before = before + count[sub : sub + 1]
    offset = jnp.concatenate(offsets, axis=0)
    for step in range(2 * groups // 8):
        rank[pl.ds(8 * step, 8), :] = rank[pl.ds(8 * step, 8), :] + offset
    most = jnp.max(before)
    full[...] = vertex[...]

    def add(turn, carry):
        row_at = lax.broadcasted_iota(jnp.int32, (rows, LANES), 0)
        col_at = lax.broadcasted_iota(jnp.int32, (cols, LANES), 0)
        ends, starts = [], [[], [], []]
        for slot in range(SLOTS):
            want = turn * SLOTS + slot
            keys = jnp.zeros((8, LANES), jnp.int32)
            pulls = jnp.zeros((8, LANES), jnp.float32)
            for step in range(2 * groups // 8):
                mine = rank[pl.ds(8 * step, 8), :] == want
                at = 8 * step % groups
                keys = keys + jnp.where(mine, key[pl.ds(8 * step, 8), :] + 1, 0)
                pulls = pulls + jnp.where(mine, pull[pl.ds(at, 8), :], 0.0)
            spot = jnp.sum(keys, axis=0, keepdims=True) - 1
            force = jnp.sum(pulls, axis=0, keepdims=True)
            row = spot >> (cols.bit_length() - 1)
            col = spot & (cols - 1)
            ends.append((row_at == row).astype(jnp.float32).astype(jnp.bfloat16))
            here = col_at == col
            rest = force
            for part in range(3):
                piece = rest.astype(jnp.bfloat16).astype(jnp.float32)
                starts[part].append(jnp.where(here, piece, 0.0).astype(jnp.bfloat16))
                rest = rest - piece
        left = jnp.concatenate(ends, axis=1)
        total = full[...]
        for part in range(3):
            total = total + lax.dot_general(
                left,
                jnp.concatenate(starts[part], axis=1),
                (((1,), (1,)), ((), ())),
                preferred_element_type=jnp.float32,
            )
        full[...] = total
        return carry

    lax.fori_loop(0, (most + SLOTS - 1) // SLOTS, add, 0)


def place(vertex, sites, classes, coupling, corner):
    groups = classes.shape[0]
    whole = pl.BlockSpec(memory_space=pltpu.VMEM)
    scalars = pl.BlockSpec(memory_space=pltpu.SMEM)
    return pl.pallas_call(
        place_kernel,
        out_shape=jax.ShapeDtypeStruct(vertex.shape, jnp.float32),
        in_specs=[scalars, scalars, whole, whole, whole],
        out_specs=whole,
        scratch_shapes=[
            pltpu.VMEM((2 * groups, LANES), jnp.int32),
            pltpu.VMEM((2 * groups, LANES), jnp.int32),
            pltpu.VMEM((groups, LANES), jnp.float32),
        ],
        compiler_params=pltpu.CompilerParams(vmem_limit_bytes=32 * 1024 * 1024),
    )(corner, coupling, sites, classes, vertex)


def gather(piece, axis, parts):
    sent = jnp.broadcast_to(piece[None], (parts, *piece.shape))
    return lax.all_to_all(sent, axis, 0, 0).reshape(parts * piece.shape[0], -1)


def scatter_sum(partial_value, axis, parts):
    pieces = partial_value.reshape(parts, partial_value.shape[0] // parts, -1)
    return jnp.sum(lax.all_to_all(pieces, axis, 0, 0), axis=0)


def make(rows_n, cols_n):
    def per_device(vertex, bubbles, site_panel, bond_sites, bond_class, coupling):
        rows_blk, cols_blk = vertex.shape
        corner = jnp.stack(
            [lax.axis_index("row") * rows_blk, lax.axis_index("col") * cols_blk]
        ).astype(jnp.int32)
        groups = bond_class.shape[0] // LANES
        sites = bond_sites.reshape(groups, LANES, 2).transpose(0, 2, 1).reshape(2 * groups, LANES)
        full = place(vertex, sites, bond_class.reshape(groups, LANES), coupling, corner)
        results = []
        current = site_panel.T
        for couple in range(2):
            known = gather(current, "col", cols_n)
            partial_value = jnp.dot(
                known, bubbles[2 * couple] * full, precision=HIGHEST, preferred_element_type=jnp.float32
            )
            odd_term = scatter_sum(partial_value, "row", rows_n)
            known = gather(odd_term, "row", rows_n)
            partial_value = lax.dot_general(
                known,
                bubbles[2 * couple + 1] * full,
                (((1,), (1,)), ((), ())),
                precision=HIGHEST,
                preferred_element_type=jnp.float32,
            )
            current = scatter_sum(partial_value, "col", cols_n)
            results += [odd_term.T, current.T]
        return tuple(results)

    return per_device


def solution(mesh):
    in_specs = (P("row", "col"), P(None, "row", "col"), P("row", "col"), P(), P(), P())
    out_specs = (P("col", "row"), P("row", "col"), P("col", "row"), P("row", "col"))
    return jax.shard_map(
        make(mesh.shape["row"], mesh.shape["col"]),
        mesh=mesh,
        in_specs=in_specs,
        out_specs=out_specs,
        check_vma=False,
    )
```

time: 735 us -> 178 us (0.24)
  the two profiles are of different devices: /device:TPU:1 before, /device:TPU:32 now
where the time goes in v1:
time: 178 us; the launch traced here: 177 us
  blocking collectives  138 us (78%)
  starting transfers between devices  15.2 us (9%)
  waiting for transfers between devices  11.9 us (7%)
  local copies, waits for them, and re-layouts  5.09 us (3%)
  matrix products  3.72 us (2%)
  Pallas kernels  2.42 us (1%)
    all_to_all x4, blocking collectives, scatter_sum(): return jnp.sum(lax.all_to_all(pieces, axis, 0, 0), axis=0)  83.3 us
    all_to_all x3, blocking collectives, gather(): return lax.all_to_all(sent, axis, 0, 0).reshape(parts * piece.shape[0], -1)  54.2 us
    all_to_all x1, starting transfers between devices, gather(): return lax.all_to_all(sent, axis, 0, 0).reshape(parts * piece.shape[0], -1)  15.2 us
    all_to_all x1, waiting for transfers between devices, gather(): return lax.all_to_all(sent, axis, 0, 0).reshape(parts * piece.shape[0], -1)  11.9 us
  transfers between devices with their start and end apart: 1, of which 1 were waited for; matrix products, arithmetic and copies ran while one was open for 0% of the time, Pallas kernels for 1%

profile of v1, /device:TPU:32, one launch (start us, length us, event | category | flops | bytes accessed | tf_op | source)
XLA Modules:
  0.0 177.4 jit_solution(9505909482569809655)
XLA Ops:
  0.6 1.4 broadcast_in_dim.8
  2.1 15.2 %all-to-all-start = ((f32[16,16,256]{2,1,0:T(8,128)}), f32[16,16,256]{2,1,0:T(8,128)S(1)}, u32[]{:S(2)}, u32[]{:S(2)}) async-start(f32[16,16,256]{2,1,0:T(8,128)} %broadcast_in_dim.8), calls=%async_computation | async-start | bytes 524288 | tf_op jit(solution)/shard_map/all_to_all | solution.py:104
  17.3 0.1 pad_add_fusion.corner
  17.4 1.0 copy-done
  18.4 0.9 copy-done.1
  19.3 0.9 copy-done.2
  20.2 0.7 copy-done.3
  20.9 2.4 %shard_map.93 = f32[256,512]{1,0:T(8,128)S(1)} custom-call(s32[2]{0:T(128)S(1)} %pad_add_fusion.corner, f32[16]{0:T(128)S(1)} %copy-done.3, s32[384,128]{1,0:T(8,128)S(1)} %bitcast.52, s32[192,128]{1,0:T(8,128)S(1)} %bitcast.53, f32[256,512]{1,0:T(8,128)S(1)} %copy-done), custom_call_target="tpu_custom_call" | custom-call | tf_op jit(solution)/shard_map/pallas_call | solution.py:88
  23.3 11.9 %all-to-all-done = f32[16,16,256]{2,1,0:T(8,128)S(1)} async-done(((f32[16,16,256]{2,1,0:T(8,128)}), f32[16,16,256]{2,1,0:T(8,128)S(1)}, u32[]{:S(2)}, u32[]{:S(2)}) %all-to-all-start) | async-done | bytes 262176 | tf_op jit(solution)/shard_map/all_to_all | solution.py:104
  35.2 1.8 %convolution_bitcast_fusion = f32[32,8,512]{2,1,0:T(8,128)S(1)} fusion(f32[256,256]{1,0:T(8,128)S(1)} %bitcast.56, f32[256,512]{1,0:T(8,128)S(1)} %shard_map.93, f32[4,256,512]{2,1,0:T(8,128)} %param.7), kind=kOutput, calls=%fused_computation | convolution fusion | flops 402784256 | bytes 1835008 | tf_op jit(solution)/shard_map/dot_general | solution.py:125
  37.0 18.9 %all_to_all.40 = f32[32,8,512]{2,1,0:T(8,128)S(1)} all-to-all(f32[32,8,512]{2,1,0:T(8,128)S(1)} %convolution_bitcast_fusion), channel_id=1, replica_groups=mesh['row'=32,'col'=16] {'row'}, dimensions={0} | all-to-all | bytes 1048576 | tf_op jit(solution)/shard_map/all_to_all | solution.py:109
  56.0 0.0 copy-start.5
  56.0 0.1 broadcast_in_dim.9
  56.0 15.2 %all_to_all.41 = f32[32,8,512]{2,1,0:T(8,128)S(1)} all-to-all(f32[32,8,512]{2,1,0:T(8,128)S(1)} %broadcast_in_dim.9), channel_id=1, replica_groups=mesh['row'=32,'col'=16] {'row'}, dimensions={0} | all-to-all | bytes 1048576 | tf_op jit(solution)/shard_map/all_to_all | solution.py:104
  71.3 0.6 fusion.4
  71.9 24.4 %all_to_all.42 = f32[16,16,256]{2,1,0:T(8,128)S(1)} all-to-all(f32[16,16,256]{2,1,0:T(8,128)S(1)} %fusion.4), channel_id=1, replica_groups=mesh['row'=32,'col'=16] {'col'}, dimensions={0} | all-to-all | bytes 524288 | tf_op jit(solution)/shard_map/all_to_all | solution.py:109
  96.3 23.8 %all_to_all.43 = f32[16,16,256]{2,1,0:T(8,128)S(1)} all-to-all(f32[16,16,256]{2,1,0:T(8,128)S(1)} %broadcast_in_dim.10), channel_id=1, replica_groups=mesh['row'=32,'col'=16] {'col'}, dimensions={0} | all-to-all | bytes 524288 | tf_op jit(solution)/shard_map/all_to_all | solution.py:104
  120.1 0.6 fusion.2
  120.8 15.8 %all_to_all.44 = f32[32,8,512]{2,1,0:T(8,128)S(1)} all-to-all(f32[32,8,512]{2,1,0:T(8,128)S(1)} %fusion.2), channel_id=1, replica_groups=mesh['row'=32,'col'=16] {'row'}, dimensions={0} | all-to-all | bytes 1048576 | tf_op jit(solution)/shard_map/all_to_all | solution.py:109
  136.6 0.1 broadcast_in_dim.11
  136.7 15.2 %all_to_all.45 = f32[32,8,512]{2,1,0:T(8,128)S(1)} all-to-all(f32[32,8,512]{2,1,0:T(8,128)S(1)} %broadcast_in_dim.11), channel_id=1, replica_groups=mesh['row'=32,'col'=16] {'row'}, dimensions={0} | all-to-all | bytes 1048576 | tf_op jit(solution)/shard_map/all_to_all | solution.py:104
  151.9 0.6 fusion
  152.6 24.2 %all_to_all.46 = f32[16,16,256]{2,1,0:T(8,128)S(1)} all-to-all(f32[16,16,256]{2,1,0:T(8,128)S(1)} %fusion), channel_id=1, replica_groups=mesh['row'=32,'col'=16] {'col'}, dimensions={0} | all-to-all | bytes 524288 | tf_op jit(solution)/shard_map/all_to_all | solution.py:109
  176.8 0.6 reduce_sum.39
  (15 shorter events, 0.2 us)
Async XLA Ops:
  2.1 33.1 %all-to-all-start = ((f32[16,16,256]{2,1,0:T(8,128)}), f32[16,16,256]{2,1,0:T(8,128)S(1)}, u32[]{:S(2)}, u32[]{:S(2)}) async-start(f32[16,16,256]{2,1,0:T(8,128)} %broadcast_in_dim.8), calls=%async_computation | async-start | bytes 524288 | tf_op jit(solution)/shard_map/all_to_all | solution.py:104
  17.4 1.0 copy-start
  18.4 0.9 copy-start.1
  19.3 0.9 copy-start.2
  20.2 0.7 copy-start.3
  35.2 36.1 %copy-start.4 = (f32[4,256,512]{2,1,0:T(8,128)S(1)}, f32[4,256,512]{2,1,0:T(8,128)}, u32[]{:S(2)}) copy-start(f32[4,256,512]{2,1,0:T(8,128)} %param.7) | copy-start | bytes 6291460
  56.0 40.3 %copy-start.5 = (f32[8,512]{1,0:T(8,128)}, f32[8,512]{1,0:T(8,128)S(1)}, u32[]{:S(2)}) copy-start(f32[8,512]{1,0:T(8,128)S(1)} %reduce_sum.36) | copy-start | bytes 49156
  96.3 40.3 %copy-start.6 = (f32[16,256]{1,0:T(8,128)}, f32[16,256]{1,0:T(8,128)S(1)}, u32[]{:S(2)}) copy-start(f32[16,256]{1,0:T(8,128)S(1)} %reduce_sum.37) | copy-start | bytes 49156
  136.6 40.8 %copy-start.7 = (f32[8,512]{1,0:T(8,128)}, f32[8,512]{1,0:T(8,128)S(1)}, u32[]{:S(2)}) copy-start(f32[8,512]{1,0:T(8,128)S(1)} %reduce_sum.38) | copy-start | bytes 49156

commit v2 on v1

--- a/solution.py
+++ b/solution.py
@@ -3,18 +3,41 @@
 from jax import lax
 from jax.experimental import pallas as pl
 from jax.experimental.pallas import tpu as pltpu
-from jax.sharding import PartitionSpec as P
+from jax.sharding import Mesh, PartitionSpec as P
 
 HIGHEST = lax.Precision.HIGHEST
 LANES = 128
 SLOTS = 8
 
 
-def place_kernel(corner, coupling, sites, classes, vertex, full, rank, key, pull):
-    rows, cols = vertex.shape
+def place_kernel(
+    corner, coupling, sites_far, classes_far, mine_far, other_far, own_far, others_far, *rest
+):
+    loops = own_far.shape[0]
+    weighted_far = rest[:loops]
+    sites, classes, full, bubbles, rank, key, pull, arrived, left_off = rest[loops:]
+    rows, cols = full.shape
+    half = rows // 2
     groups = classes.shape[0]
-    first = sites[pl.ds(0, groups, stride=2), :] if sites.ndim == 2 else sites[0]
-    second = sites[pl.ds(1, groups, stride=2), :] if sites.ndim == 2 else sites[1]
+    copies = [
+        pltpu.make_async_copy(far, near, arrived.at[index])
+        for index, (far, near) in enumerate(
+            (
+                (sites_far, sites),
+                (classes_far, classes),
+                (mine_far, full.at[pl.ds(0, half)]),
+                (other_far, full.at[pl.ds(half, half)]),
+                (own_far, bubbles.at[:, pl.ds(0, half)]),
+                (others_far, bubbles.at[:, pl.ds(half, half)]),
+            )
+        )
+    ]
+    for copy in copies:
+        copy.start()
+    copies[0].wait()
+    copies[1].wait()
+    first = sites[pl.ds(0, groups, stride=2), :]
+    second = sites[pl.ds(1, groups, stride=2), :]
     kind = classes[...]
     strength = jnp.zeros(kind.shape, jnp.float32)
     for index in range(coupling.shape[0]):
@@ -25,7 +48,7 @@
         row = end - corner[0]
         col = start - corner[1]
         inside = (row >= 0) & (row < rows) & (col >= 0) & (col < cols)
-        key[pl.ds(way * groups, groups), :] = row * cols + col
+        key[pl.ds(way * groups, groups), :] = (row ^ corner[2]) * cols + col
         hit = inside.astype(jnp.int32)
         for step in range(groups // 8):
             now = hit[8 * step : 8 * step + 8]
@@ -40,7 +63,8 @@
     for step in range(2 * groups // 8):
         rank[pl.ds(8 * step, 8), :] = rank[pl.ds(8 * step, 8), :] + offset
     most = jnp.max(before)
-    full[...] = vertex[...]
+    copies[2].wait()
+    copies[3].wait()
 
     def add(turn, carry):
         row_at = lax.broadcasted_iota(jnp.int32, (rows, LANES), 0)
@@ -79,24 +103,41 @@
         return carry
 
     lax.fori_loop(0, (most + SLOTS - 1) // SLOTS, add, 0)
-
-
-def place(vertex, sites, classes, coupling, corner):
+    copies[4].wait()
+    copies[5].wait()
+    leaving = []
+    for step in range(loops):
+        bubbles[step] = bubbles[step] * full[...]
+        leaving.append(pltpu.make_async_copy(bubbles.at[step], weighted_far[step], left_off.at[step]))
+        leaving[-1].start()
+    for copy in leaving:
+        copy.wait()
+
+
+def place(vertex, other_vertex, bubbles, other_bubbles, sites, classes, coupling, corner):
+    half, cols = vertex.shape
     groups = classes.shape[0]
-    whole = pl.BlockSpec(memory_space=pltpu.VMEM)
+    far = pl.BlockSpec(memory_space=pl.ANY)
     scalars = pl.BlockSpec(memory_space=pltpu.SMEM)
+    loops = bubbles.shape[0]
     return pl.pallas_call(
         place_kernel,
-        out_shape=jax.ShapeDtypeStruct(vertex.shape, jnp.float32),
-        in_specs=[scalars, scalars, whole, whole, whole],
-        out_specs=whole,
+        out_shape=[jax.ShapeDtypeStruct((2 * half, cols), jnp.float32)] * loops,
+        in_specs=[scalars, scalars] + [far] * 6,
+        out_specs=[far] * loops,
         scratch_shapes=[
+            pltpu.VMEM(sites.shape, jnp.int32),
+            pltpu.VMEM(classes.shape, jnp.int32),
+            pltpu.VMEM((2 * half, cols), jnp.float32),
+            pltpu.VMEM((loops, 2 * half, cols), jnp.float32),
             pltpu.VMEM((2 * groups, LANES), jnp.int32),
             pltpu.VMEM((2 * groups, LANES), jnp.int32),
             pltpu.VMEM((groups, LANES), jnp.float32),
+            pltpu.SemaphoreType.DMA((6,)),
+            pltpu.SemaphoreType.DMA((loops,)),
         ],
-        compiler_params=pltpu.CompilerParams(vmem_limit_bytes=32 * 1024 * 1024),
-    )(corner, coupling, sites, classes, vertex)
+        compiler_params=pltpu.CompilerParams(vmem_limit_bytes=59 * 1024 * 1024),
+    )(corner, coupling, sites, classes, vertex, other_vertex, bubbles, other_bubbles)
 
 
 def gather(piece, axis, parts):
@@ -109,45 +150,71 @@
     return jnp.sum(lax.all_to_all(pieces, axis, 0, 0), axis=0)
 
 
-def make(rows_n, cols_n):
+def make(chips, cols_n):
+    swap = [(0, 1), (1, 0)]
+
     def per_device(vertex, bubbles, site_panel, bond_sites, bond_class, coupling):
-        rows_blk, cols_blk = vertex.shape
+        half, cols_blk = vertex.shape
+        core = lax.axis_index("core")
         corner = jnp.stack(
-            [lax.axis_index("row") * rows_blk, lax.axis_index("col") * cols_blk]
+            [lax.axis_index("chip") * 2 * half, lax.axis_index("col") * cols_blk, core * half]
         ).astype(jnp.int32)
         groups = bond_class.shape[0] // LANES
         sites = bond_sites.reshape(groups, LANES, 2).transpose(0, 2, 1).reshape(2 * groups, LANES)
-        full = place(vertex, sites, bond_class.reshape(groups, LANES), coupling, corner)
-        results = []
-        current = site_panel.T
+        panels = lax.all_gather(site_panel.T, "core")
+        wide = panels.reshape(2, 2, panels.shape[1] // 2, half)
+        held = jnp.where(core == 0, wide[:, 0], wide[:, 1])
+        current = jnp.where(
+            core == 0,
+            jnp.concatenate([held[0], held[1]], axis=1),
+            jnp.concatenate([held[1], held[0]], axis=1),
+        )
+        sent = jnp.broadcast_to(current[None], (cols_n, *current.shape))
+        sent, sent_vertex, sent_bubbles = lax.optimization_barrier((sent, vertex, bubbles))
+        known = lax.all_to_all(sent, "col", 0, 0).reshape(-1, 2 * half)
+        weighted = place(
+            vertex,
+            lax.ppermute(sent_vertex, "core", swap),
+            bubbles,
+            lax.ppermute(sent_bubbles, "core", swap),
+            sites,
+            bond_class.reshape(groups, LANES),
+            coupling,
+            corner,
+        )
+        odd_terms, even_terms = [], []
         for couple in range(2):
-            known = gather(current, "col", cols_n)
             partial_value = jnp.dot(
-                known, bubbles[2 * couple] * full, precision=HIGHEST, preferred_element_type=jnp.float32
-            )
-            odd_term = scatter_sum(partial_value, "row", rows_n)
-            known = gather(odd_term, "row", rows_n)
+                known, weighted[2 * couple], precision=HIGHEST, preferred_element_type=jnp.float32
+            )
+            odd_term = scatter_sum(partial_value, "chip", chips)
+            odd_terms.append(odd_term.T)
             partial_value = lax.dot_general(
-                known,
-                bubbles[2 * couple + 1] * full,
+                gather(odd_term, "chip", chips),
+                weighted[2 * couple + 1],
                 (((1,), (1,)), ((), ())),
                 precision=HIGHEST,
                 preferred_element_type=jnp.float32,
             )
             current = scatter_sum(partial_value, "col", cols_n)
-            results += [odd_term.T, current.T]
-        return tuple(results)
+            even_terms.append(current)
+            if couple == 0:
+                known = gather(current, "col", cols_n)
+        both = lax.all_gather(jnp.stack(even_terms), "core")
+        swapped = jnp.where(core == 0, both[0, :, :, :half], both[0, :, :, half:])
+        straight = jnp.where(core == 0, both[1, :, :, half:], both[1, :, :, :half])
+        even_terms = jnp.concatenate([swapped, straight], axis=1)
+        return odd_terms[0], even_terms[0].T, odd_terms[1], even_terms[1].T
 
     return per_device
 
 
 def solution(mesh):
-    in_specs = (P("row", "col"), P(None, "row", "col"), P("row", "col"), P(), P(), P())
-    out_specs = (P("col", "row"), P("row", "col"), P("col", "row"), P("row", "col"))
+    chips, cols_n = mesh.shape["row"] // 2, mesh.shape["col"]
+    inner = Mesh(mesh.devices.reshape(chips, 2, cols_n), ("chip", "core", "col"))
+    row = ("chip", "core")
+    in_specs = (P(row, "col"), P(None, row, "col"), P(row, "col"), P(), P(), P())
+    out_specs = (P("col", row), P(row, "col"), P("col", row), P(row, "col"))
     return jax.shard_map(
-        make(mesh.shape["row"], mesh.shape["col"]),
-        mesh=mesh,
-        in_specs=in_specs,
-        out_specs=out_specs,
-        check_vma=False,
+        make(chips, cols_n), mesh=inner, in_specs=in_specs, out_specs=out_specs, check_vma=False
     )

time: 178 us -> 166 us (0.933)
  the two profiles are of different devices: /device:TPU:32 before, /device:TPU:1 now
where the time goes in v2:
time: 166 us; the launch traced here: 165 us
  blocking collectives  132 us (80%)
  starting transfers between devices  14.2 us (9%)
  Pallas kernels  6.42 us (4%)
  matrix products  5 us (3%)
  waiting for transfers between devices  3.3 us (2%)
  local copies, waits for them, and re-layouts  2.32 us (1%)
    all_to_all x4, blocking collectives, scatter_sum(): return jnp.sum(lax.all_to_all(pieces, axis, 0, 0), axis=0)  70.8 us
    all_to_all x3, blocking collectives, gather(): return lax.all_to_all(sent, axis, 0, 0).reshape(parts * piece.shape[0], -1)  42.2 us
    all_gather x1, blocking collectives, per_device(): both = lax.all_gather(jnp.stack(even_terms), 'core')  10.1 us
    all_to_all x1, starting transfers between devices, per_device(): known = lax.all_to_all(sent, 'col', 0, 0).reshape(-1, 2 * half)  9.55 us
    all_gather x1, blocking collectives, per_device(): panels = lax.all_gather(site_panel.T, 'core')  8.58 us
    pallas_call x1, Pallas kernels, place(): pl.pallas_call(place_kernel, out_shape=[jax.ShapeDtypeStruct((2 * half, c...  6.42 us
  transfers between devices with their start and end apart: 3, of which 2 were waited for; matrix products, arithmetic and copies ran while one was open for 0% of the time, Pallas kernels for 4%

profile of v2, /device:TPU:1, one launch (start us, length us, event | category | flops | bytes accessed | tf_op | source)
XLA Modules:
  0.0 164.9 jit_solution(24108121292642517)
XLA Ops:
  0.6 8.6 %all-gather = f32[32,256]{1,0:T(8,128)S(1)} all-gather(f32[16,256]{1,0:T(8,128)} %bitcast.56), channel_id=2, replica_groups=mesh['chip'=16,'core'=2,'col'=16] {'core'}, dimensions={0}, use_global_device_ids=true | all-gather | bytes 49152 | tf_op jit(solution)/shard_map/all_gather | solution.py:164
  9.2 0.7 broadcast_in_dim.8
  10.0 2.2 %collective-permute-start.1 = (f32[4,256,512]{2,1,0:T(8,128)}, f32[4,256,512]{2,1,0:T(8,128)S(1)}, u32[]{:S(2)}, u32[]{:S(2)}) collective-permute-start(f32[4,256,512]{2,1,0:T(8,128)} %own_far.1), channel_id=1, source_target_pairs={{0,16},{16,0},{1,17},{17,1},{2,18},{18,2},{3,19},{19,3},{4,20},{20... | collective-permute-start | bytes 6291464 | tf_op jit(solution)/shard_map/ppermute | solution.py:179
  12.2 9.6 %all-to-all-start = ((f32[16,8,512]{2,1,0:T(8,128)}), f32[16,8,512]{2,1,0:T(8,128)S(1)}, u32[]{:S(2)}, u32[]{:S(2)}) async-start(f32[16,8,512]{2,1,0:T(8,128)} %broadcast_in_dim.8), calls=%async_computation | async-start | bytes 524288 | tf_op jit(solution)/shard_map/all_to_all | solution.py:174
  21.8 2.4 %collective-permute-start = (f32[256,512]{1,0:T(8,128)}, f32[256,512]{1,0:T(8,128)S(1)}, u32[]{:S(2)}, u32[]{:S(2)}) collective-permute-start(f32[256,512]{1,0:T(8,128)} %mine_far.1), channel_id=1, source_target_pairs={{0,16},{16,0},{1,17},{17,1},{2,18},{18,2},{3,19},{19,3},{4,20},{20... | collective-permute-start | bytes 1572872 | tf_op jit(solution)/shard_map/ppermute | solution.py:177
  24.2 0.6 pad_add_fusion.corner
  24.8 1.1 collective-permute-done.other_far
  25.9 0.8 copy-done.4
  26.7 0.7 copy-done
  27.4 6.4 %shard_map.93 = (f32[512,512]{1,0:T(8,128)}, f32[512,512]{1,0:T(8,128)}, f32[512,512]{1,0:T(8,128)}, f32[512,512]{1,0:T(8,128)}) custom-call(s32[3]{0:T(128)} %pad_add_fusion.corner, f32[16]{0:T(128)} %coupling.1, s32[384,128]{1,0:T(8,128)} %bitcast.49, s32[192,128]{1,0:T(8,128)} %bitcast.52, f32[256,512]{1,0:T(8,128)} %mine_far.1, f32[256,512]{1,0:T(8,128)} %copy-done.4, ...), custom_call_target="tpu_custom_call" | custom-call | tf_op jit(solution)/shard_map/pallas_call | solution.py:123
  33.8 2.2 %all-to-all-done = f32[16,8,512]{2,1,0:T(8,128)S(1)} async-done(((f32[16,8,512]{2,1,0:T(8,128)}), f32[16,8,512]{2,1,0:T(8,128)S(1)}, u32[]{:S(2)}, u32[]{:S(2)}) %all-to-all-start) | async-done | bytes 262176 | tf_op jit(solution)/shard_map/all_to_all | solution.py:174
  36.0 1.9 %fusion.6 = f32[16,8,512]{2,1,0:T(8,128)S(1)} fusion(f32[16,8,512]{2,1,0:T(8,128)S(1)} %all-to-all-done, f32[512,512]{1,0:T(8,128)} %get-tuple-element.14), kind=kOutput, calls=%fused_computation.6 | convolution fusion | flops 402653184 | bytes 1572864 | tf_op jit(solution)/shard_map/dot_general | solution.py:187
  37.9 14.1 %all_to_all.40 = f32[16,8,512]{2,1,0:T(8,128)S(1)} all-to-all(f32[16,8,512]{2,1,0:T(8,128)S(1)} %fusion.6), channel_id=1, replica_groups=mesh['chip'=16,'core'=2,'col'=16] {'chip'}, dimensions={0} | all-to-all | bytes 524288 | tf_op jit(solution)/shard_map/all_to_all | solution.py:150
  52.1 10.3 %all_to_all.41 = f32[16,8,512]{2,1,0:T(8,128)S(1)} all-to-all(f32[16,8,512]{2,1,0:T(8,128)S(1)} %broadcast_in_dim.9), channel_id=1, replica_groups=mesh['chip'=16,'core'=2,'col'=16] {'chip'}, dimensions={0} | all-to-all | bytes 524288 | tf_op jit(solution)/shard_map/all_to_all | solution.py:145
  62.4 1.2 fusion.4
  63.6 22.9 %all_to_all.42 = f32[16,8,512]{2,1,0:T(8,128)S(1)} all-to-all(f32[16,8,512]{2,1,0:T(8,128)S(1)} %fusion.4), channel_id=1, replica_groups=mesh['chip'=16,'core'=2,'col'=16] {'col'}, dimensions={0} | all-to-all | bytes 524288 | tf_op jit(solution)/shard_map/all_to_all | solution.py:150
  86.6 21.7 %all_to_all.43 = f32[16,8,512]{2,1,0:T(8,128)S(1)} all-to-all(f32[16,8,512]{2,1,0:T(8,128)S(1)} %broadcast_in_dim.10), channel_id=1, replica_groups=mesh['chip'=16,'core'=2,'col'=16] {'col'}, dimensions={0} | all-to-all | bytes 524288 | tf_op jit(solution)/shard_map/all_to_all | solution.py:145
  108.3 0.7 fusion.2
  109.0 10.8 %all_to_all.44 = f32[16,8,512]{2,1,0:T(8,128)S(1)} all-to-all(f32[16,8,512]{2,1,0:T(8,128)S(1)} %fusion.2), channel_id=1, replica_groups=mesh['chip'=16,'core'=2,'col'=16] {'chip'}, dimensions={0} | all-to-all | bytes 524288 | tf_op jit(solution)/shard_map/all_to_all | solution.py:150
  119.9 10.2 %all_to_all.45 = f32[16,8,512]{2,1,0:T(8,128)S(1)} all-to-all(f32[16,8,512]{2,1,0:T(8,128)S(1)} %broadcast_in_dim.11), channel_id=1, replica_groups=mesh['chip'=16,'core'=2,'col'=16] {'chip'}, dimensions={0} | all-to-all | bytes 524288 | tf_op jit(solution)/shard_map/all_to_all | solution.py:145
  130.1 1.2 fusion
  131.3 22.9 %all_to_all.46 = f32[16,8,512]{2,1,0:T(8,128)S(1)} all-to-all(f32[16,8,512]{2,1,0:T(8,128)S(1)} %fusion), channel_id=1, replica_groups=mesh['chip'=16,'core'=2,'col'=16] {'col'}, dimensions={0} | all-to-all | bytes 524288 | tf_op jit(solution)/shard_map/all_to_all | solution.py:150
  154.2 10.1 %all-gather.1 = f32[4,8,512]{2,1,0:T(8,128)S(1)} all-gather(f32[2,8,512]{2,1,0:T(8,128)S(1)} %pad_maximum_fusion), channel_id=3, replica_groups=mesh['chip'=16,'core'=2,'col'=16] {'core'}, dimensions={0}, use_global_device_ids=true | all-gather | bytes 98304 | tf_op jit(solution)/shard_map/all_gather | solution.py:203
  164.3 0.6 fusion.10
  (25 shorter events, 0.2 us)
Async XLA Ops:
  10.0 15.9 %collective-permute-start.1 = (f32[4,256,512]{2,1,0:T(8,128)}, f32[4,256,512]{2,1,0:T(8,128)S(1)}, u32[]{:S(2)}, u32[]{:S(2)}) collective-permute-start(f32[4,256,512]{2,1,0:T(8,128)} %own_far.1), channel_id=1, source_target_pairs={{0,16},{16,0},{1,17},{17,1},{2,18},{18,2},{3,19},{19,3},{4,20},{20... | collective-permute-start | bytes 6291464 | tf_op jit(solution)/shard_map/ppermute | solution.py:179
  12.2 23.8 %all-to-all-start = ((f32[16,8,512]{2,1,0:T(8,128)}), f32[16,8,512]{2,1,0:T(8,128)S(1)}, u32[]{:S(2)}, u32[]{:S(2)}) async-start(f32[16,8,512]{2,1,0:T(8,128)} %broadcast_in_dim.8), calls=%async_computation | async-start | bytes 524288 | tf_op jit(solution)/shard_map/all_to_all | solution.py:174
  21.8 4.1 %collective-permute-start = (f32[256,512]{1,0:T(8,128)}, f32[256,512]{1,0:T(8,128)S(1)}, u32[]{:S(2)}, u32[]{:S(2)}) collective-permute-start(f32[256,512]{1,0:T(8,128)} %mine_far.1), channel_id=1, source_target_pairs={{0,16},{16,0},{1,17},{17,1},{2,18},{18,2},{3,19},{19,3},{4,20},{20... | collective-permute-start | bytes 1572872 | tf_op jit(solution)/shard_map/ppermute | solution.py:177
  25.9 0.8 copy-start.4
  25.9 1.5 copy-start
  33.8 28.6 %copy-start.3 = (f32[512,512]{1,0:T(8,128)S(1)}, f32[512,512]{1,0:T(8,128)}, u32[]{:S(2)}) copy-start(f32[512,512]{1,0:T(8,128)} %get-tuple-element.15) | copy-start | bytes 3145732
  52.0 56.3 %copy-start.2 = (f32[512,512]{1,0:T(8,128)S(1)}, f32[512,512]{1,0:T(8,128)}, u32[]{:S(2)}) copy-start(f32[512,512]{1,0:T(8,128)} %get-tuple-element.16) | copy-start | bytes 3145732
  52.1 57.0 %copy-start.5 = (f32[8,512]{1,0:T(8,128)}, f32[8,512]{1,0:T(8,128)S(1)}, u32[]{:S(2)}) copy-start(f32[8,512]{1,0:T(8,128)S(1)} %reduce_sum.36) | copy-start | bytes 49156
  86.5 43.6 %copy-start.1 = (f32[512,512]{1,0:T(8,128)S(1)}, f32[512,512]{1,0:T(8,128)}, u32[]{:S(2)}) copy-start(f32[512,512]{1,0:T(8,128)} %get-tuple-element.17) | copy-start | bytes 3145732
  119.9 45.0 %copy-start.6 = (f32[8,512]{1,0:T(8,128)}, f32[8,512]{1,0:T(8,128)S(1)}, u32[]{:S(2)}) copy-start(f32[8,512]{1,0:T(8,128)S(1)} %reduce_sum.38) | copy-start | bytes 49156

commit v3 on v2

v3 whole, which is shorter than its diff:
```python
import jax
import jax.numpy as jnp
from jax import lax
from jax.experimental import pallas as pl
from jax.experimental.pallas import tpu as pltpu
from jax.sharding import Mesh, PartitionSpec as P

HIGHEST = lax.Precision.HIGHEST
LANES = 128
SLOTS = 8


def fetch(pairs, arrived):
    copies = [
        pltpu.make_async_copy(far, near, arrived.at[index]) for index, (far, near) in enumerate(pairs)
    ]
    for copy in copies:
        copy.start()
    return copies


def place_kernel(
    corner, coupling, sites_far, classes_far, vertex_far, full, sites, classes, rank, key, pull, arrived
):
    rows, cols = full.shape
    groups = classes.shape[0]
    copies = fetch(((sites_far, sites), (classes_far, classes), (vertex_far, full)), arrived)
    copies[0].wait()
    copies[1].wait()
    first = sites[pl.ds(0, groups, stride=2), :]
    second = sites[pl.ds(1, groups, stride=2), :]
    kind = classes[...]
    strength = jnp.zeros(kind.shape, jnp.float32)
    for index in range(coupling.shape[0]):
        strength = jnp.where(kind == index, coupling[index], strength)
    pull[...] = strength
    count = jnp.zeros((8, LANES), jnp.int32)
    for way, (end, start) in enumerate(((first, second), (second, first))):
        row = end - corner[0]
        col = start - corner[1]
        inside = (row >= 0) & (row < rows) & (col >= 0) & (col < cols)
        key[pl.ds(way * groups, groups), :] = row * cols + col
        hit = inside.astype(jnp.int32)
        for step in range(groups // 8):
            now = hit[8 * step : 8 * step + 8]
            rank[pl.ds(way * groups + 8 * step, 8), :] = jnp.where(now == 1, count, -(1 << 20))
            count = count + now
    before = jnp.zeros((1, LANES), jnp.int32)
    offsets = []
    for sub in range(8):
        offsets.append(before)
        before = before + count[sub : sub + 1]
    offset = jnp.concatenate(offsets, axis=0)
    for step in range(2 * groups // 8):
        rank[pl.ds(8 * step, 8), :] = rank[pl.ds(8 * step, 8), :] + offset
    most = jnp.max(before)
    copies[2].wait()

    def add(turn, carry):
        row_at = lax.broadcasted_iota(jnp.int32, (rows, LANES), 0)
        col_at = lax.broadcasted_iota(jnp.int32, (cols, LANES), 0)
        ends, starts = [], [[], [], []]
        for slot in range(SLOTS):
            want = turn * SLOTS + slot
            keys = jnp.zeros((8, LANES), jnp.int32)
            pulls = jnp.zeros((8, LANES), jnp.float32)
            for step in range(2 * groups // 8):
                mine = rank[pl.ds(8 * step, 8), :] == want
                at = 8 * step % groups
                keys = keys + jnp.where(mine, key[pl.ds(8 * step, 8), :] + 1, 0)
                pulls = pulls + jnp.where(mine, pull[pl.ds(at, 8), :], 0.0)
            spot = jnp.sum(keys, axis=0, keepdims=True) - 1
            force = jnp.sum(pulls, axis=0, keepdims=True)
            row = spot >> (cols.bit_length() - 1)
            col = spot & (cols - 1)
            ends.append((row_at == row).astype(jnp.float32).astype(jnp.bfloat16))
            here = col_at == col
            rest = force
            for part in range(3):
                piece = rest.astype(jnp.bfloat16).astype(jnp.float32)
                starts[part].append(jnp.where(here, piece, 0.0).astype(jnp.bfloat16))
                rest = rest - piece
        left = jnp.concatenate(ends, axis=1)
        total = full[...]
        for part in range(3):
            total = total + lax.dot_general(
                left,
                jnp.concatenate(starts[part], axis=1),
                (((1,), (1,)), ((), ())),
                preferred_element_type=jnp.float32,
            )
        full[...] = total
        return carry

    lax.fori_loop(0, (most + SLOTS - 1) // SLOTS, add, 0)


def place(vertex, sites, classes, coupling, corner):
    groups = classes.shape[0]
    far = pl.BlockSpec(memory_space=pl.ANY)
    scalars = pl.BlockSpec(memory_space=pltpu.SMEM)
    sites, classes, vertex = (
        pltpu.with_memory_space_constraint(array, pltpu.HBM) for array in (sites, classes, vertex)
    )
    return pl.pallas_call(
        place_kernel,
        out_shape=pltpu.VMEM(vertex.shape, jnp.float32),
        in_specs=[scalars, scalars] + [far] * 3,
        out_specs=pl.BlockSpec(memory_space=pltpu.VMEM),
        scratch_shapes=[
            pltpu.VMEM(sites.shape, jnp.int32),
            pltpu.VMEM(classes.shape, jnp.int32),
            pltpu.VMEM((2 * groups, LANES), jnp.int32),
            pltpu.VMEM((2 * groups, LANES), jnp.int32),
            pltpu.VMEM((groups, LANES), jnp.float32),
            pltpu.SemaphoreType.DMA((3,)),
        ],
        cost_estimate=pl.CostEstimate(flops=20 * 10**9, bytes_accessed=10**6, transcendentals=0),
        compiler_params=pltpu.CompilerParams(vmem_limit_bytes=24 * 1024 * 1024),
    )(corner, coupling, sites, classes, vertex)


def weigh_kernel(own_full, other_full, own_far, others_far, *rest):
    loops, half = own_far.shape[:2]
    weighted_far, (weighted, bubbles, gone, arrived) = rest[:loops], rest[loops:]
    copies = fetch(
        [
            (far.at[step], bubbles.at[step, pl.ds(half * index, half)])
            for step in range(loops)
            for index, far in enumerate((own_far, others_far))
        ],
        arrived,
    )
    leaving = []
    for step in range(loops):
        for index, full in enumerate((own_full, other_full)):
            copies[2 * step + index].wait()
            rows = pl.ds(half * index, half)
            product = bubbles[step, rows, :] * full[...]
            if step % 2:
                weighted[step, :, rows] = product.T
            else:
                weighted[step, rows, :] = product
        leaving.append(pltpu.make_async_copy(weighted.at[step], weighted_far[step], gone.at[step]))
        leaving[-1].start()
    for copy in leaving:
        copy.wait()


def weigh(own_full, other_full, bubbles, other_bubbles):
    loops, half, cols = bubbles.shape
    near = pl.BlockSpec(memory_space=pltpu.VMEM)
    far = pl.BlockSpec(memory_space=pl.ANY)
    return pl.pallas_call(
        weigh_kernel,
        out_shape=[jax.ShapeDtypeStruct((2 * half, cols), jnp.float32)] * loops,
        in_specs=[near, near, far, far],
        out_specs=[far] * loops,
        scratch_shapes=[
            pltpu.VMEM((loops, 2 * half, cols), jnp.float32),
            pltpu.VMEM((loops, 2 * half, cols), jnp.float32),
            pltpu.SemaphoreType.DMA((loops,)),
            pltpu.SemaphoreType.DMA((2 * loops,)),
        ],
        cost_estimate=pl.CostEstimate(
            flops=2 * loops * half * cols, bytes_accessed=16 * loops * half * cols, transcendentals=0
        ),
        compiler_params=pltpu.CompilerParams(vmem_limit_bytes=24 * 1024 * 1024),
    )(own_full, other_full, pltpu.with_memory_space_constraint(bubbles, pltpu.HBM), other_bubbles)


def product_kernel(known, weighted, out):
    product = jnp.dot(
        known[...].reshape(-1, known.shape[2]),
        weighted[...],
        precision=HIGHEST,
        preferred_element_type=jnp.float32,
    )
    out[...] = product.reshape(out.shape)


def product(known, weighted):
    near = pl.BlockSpec(memory_space=pltpu.VMEM)
    return pl.pallas_call(
        product_kernel,
        out_shape=jax.ShapeDtypeStruct(known.shape, jnp.float32),
        in_specs=[near, near],
        out_specs=near,
        compiler_params=pltpu.CompilerParams(vmem_limit_bytes=16 * 1024 * 1024),
    )(known, weighted)


def gather(piece, axis, parts):
    return lax.all_to_all(jnp.broadcast_to(piece[None], (parts, *piece.shape)), axis, 0, 0)


def scatter_sum(pieces, axis):
    return jnp.sum(lax.all_to_all(pieces, axis, 0, 0), axis=0)


def make(chips, cols_n):
    swap = [(0, 1), (1, 0)]

    def per_device(vertex, bubbles, site_panel, bond_sites, bond_class, coupling):
        half, cols_blk = vertex.shape
        core = lax.axis_index("core")
        corner = jnp.stack(
            [lax.axis_index(("chip", "core")) * half, lax.axis_index("col") * cols_blk]
        ).astype(jnp.int32)
        groups = bond_class.shape[0] // LANES
        sites = bond_sites.reshape(groups, LANES, 2).transpose(0, 2, 1).reshape(2 * groups, LANES)
        panels = lax.all_gather(site_panel.T, "core")
        wide = panels.reshape(2, 2, panels.shape[1] // 2, half)
        held = jnp.where(core == 0, wide[:, 0], wide[:, 1])
        current = jnp.where(
            core == 0,
            jnp.concatenate([held[0], held[1]], axis=1),
            jnp.concatenate([held[1], held[0]], axis=1),
        )
        sent = jnp.broadcast_to(current[None], (cols_n, *current.shape))
        sent, corner, sent_bubbles = lax.optimization_barrier((sent, corner, bubbles))
        known = lax.all_to_all(sent, "col", 0, 0)
        full = place(vertex, sites, bond_class.reshape(groups, LANES), coupling, corner)
        weighted = weigh(
            full,
            lax.ppermute(full, "core", swap),
            bubbles,
            lax.ppermute(sent_bubbles, "core", swap),
        )
        first = scatter_sum(product(known, weighted[0]), "chip")
        second = scatter_sum(product(gather(first, "chip", chips), weighted[1]), "col")
        third = scatter_sum(product(gather(second, "col", cols_n), weighted[2]), "chip")
        fourth = scatter_sum(product(gather(third, "chip", chips), weighted[3]), "col")
        both = lax.all_gather(jnp.stack([second, fourth]), "core")
        swapped = jnp.where(core == 0, both[0, :, :, :half], both[0, :, :, half:])
        straight = jnp.where(core == 0, both[1, :, :, half:], both[1, :, :, :half])
        even_terms = jnp.concatenate([swapped, straight], axis=1)
        return first.T, even_terms[0].T, third.T, even_terms[1].T

    return per_device


def solution(mesh):
    chips, cols_n = mesh.shape["row"] // 2, mesh.shape["col"]
    inner = Mesh(mesh.devices.reshape(chips, 2, cols_n), ("chip", "core", "col"))
    row = ("chip", "core")
    in_specs = (P(row, "col"), P(None, row, "col"), P(row, "col"), P(), P(), P())
    out_specs = (P("col", row), P(row, "col"), P("col", row), P(row, "col"))
    return jax.shard_map(
        make(chips, cols_n), mesh=inner, in_specs=in_specs, out_specs=out_specs, check_vma=False
    )
```

time: 166 us -> 164 us (0.988)
  matrix products: 5 us -> 0 us
  Pallas kernels: 6.42 us -> 8.56 us
  blocking collectives: 132 us -> 134 us
    dot_general x4 -> x0, matrix products: 5 us -> none  [the longest x2 2.65 us: per_device(): jnp.dot(known, weighted[2 * couple], precision=HIGHEST, preferred_element...]
    pallas_call x1 -> x6, Pallas kernels: 6.42 us -> 8.56 us  [the longest x1 3.45 us: place(): pl.pallas_call(place_kernel, out_shape=pltpu.VMEM(vertex.shape, jnp.float...]
    all_to_all x1, waiting for transfers between devices: 2.17 us -> 0.08 us  [per_device(): known = lax.all_to_all(sent, 'col', 0, 0)]
where the time goes in v3:
time: 164 us
  blocking collectives  134 us (82%)
  starting transfers between devices  14 us (9%)
  Pallas kernels  8.56 us (5%)
  local copies, waits for them, and re-layouts  3.67 us (2%)
  waiting for transfers between devices  1.96 us (1%)
    all_to_all x4, blocking collectives, scatter_sum(): return jnp.sum(lax.all_to_all(pieces, axis, 0, 0), axis=0)  72.3 us
    all_to_all x3, blocking collectives, gather(): lax.all_to_all(jnp.broadcast_to(piece[None], (parts, *piece.shape)), axis...  42.9 us
    all_gather x1, blocking collectives, per_device(): both = lax.all_gather(jnp.stack([second, fourth]), 'core')  10 us
    all_to_all x1, starting transfers between devices, per_device(): known = lax.all_to_all(sent, 'col', 0, 0)  9.54 us
    all_gather x1, blocking collectives, per_device(): panels = lax.all_gather(site_panel.T, 'core')  8.58 us
    pallas_call x1, Pallas kernels, place(): pl.pallas_call(place_kernel, out_shape=pltpu.VMEM(vertex.shape, jnp.float...  3.45 us
  transfers between devices with their start and end apart: 3, of which 2 were waited for; matrix products, arithmetic and copies ran while one was open for 0% of the time, Pallas kernels for 4%

profile of v3, /device:TPU:1, one launch (start us, length us, event | category | flops | bytes accessed | tf_op | source)
XLA Modules:
  0.0 163.7 jit_solution(14961408250394606030)
XLA Ops:
  0.6 8.6 %all-gather = f32[32,256]{1,0:T(8,128)S(1)} all-gather(f32[16,256]{1,0:T(8,128)} %bitcast.37), channel_id=2, replica_groups=mesh['chip'=16,'core'=2,'col'=16] {'core'}, dimensions={0}, use_global_device_ids=true | all-gather | bytes 49152 | tf_op jit(solution)/shard_map/all_gather | solution.py:212
  9.3 0.7 broadcast_in_dim.8
  10.1 9.5 %all-to-all-start = ((f32[16,8,512]{2,1,0:T(8,128)}), f32[16,8,512]{2,1,0:T(8,128)S(1)}, u32[]{:S(2)}, u32[]{:S(2)}) async-start(f32[16,8,512]{2,1,0:T(8,128)} %broadcast_in_dim.8), calls=%async_computation | async-start | bytes 524288 | tf_op jit(solution)/shard_map/all_to_all | solution.py:222
  19.6 2.5 %collective-permute-start.1 = (f32[4,256,512]{2,1,0:T(8,128)}, f32[4,256,512]{2,1,0:T(8,128)S(1)}, u32[]{:S(2)}, u32[]{:S(2)}) collective-permute-start(f32[4,256,512]{2,1,0:T(8,128)} %own_far.1), channel_id=1, source_target_pairs={{0,16},{16,0},{1,17},{17,1},{2,18},{18,2},{3,19},{19,3},{4,20},{20... | collective-permute-start | bytes 6291464 | tf_op jit(solution)/shard_map/ppermute | solution.py:228
  22.2 0.6 copy-done.2
  22.8 3.4 %shard_map.93.own_full = f32[256,512]{1,0:T(8,128)S(1)} custom-call(s32[2]{0:T(128)S(1)} %pad_add_fusion.corner, f32[16]{0:T(128)S(1)} %copy-done.2, s32[384,128]{1,0:T(8,128)} %bitcast.38, s32[192,128]{1,0:T(8,128)} %bitcast.39, f32[256,512]{1,0:T(8,128)} %vertex_far.1), custom_call_target="tpu_custom_call" | custom-call | flops 20000000000 | bytes 1000000 | tf_op jit(solution)/shard_map/pallas_call | solution.py:105
  26.3 1.9 %collective-permute-start = (f32[256,512]{1,0:T(8,128)S(1)}, f32[256,512]{1,0:T(8,128)S(1)}, u32[]{:S(2)}, u32[]{:S(2)}) collective-permute-start(f32[256,512]{1,0:T(8,128)S(1)} %shard_map.93.own_full), channel_id=1, source_target_pairs={{0,16},{16,0},{1,17},{17,1},{2,18},{18,2},{3,19},{19,3},{4,20},{20... | collective-permute-start | bytes 1572872 | tf_op jit(solution)/shard_map/ppermute | solution.py:226
  28.2 1.9 %collective-permute-done.other_full = f32[256,512]{1,0:T(8,128)S(1)} collective-permute-done((f32[256,512]{1,0:T(8,128)S(1)}, f32[256,512]{1,0:T(8,128)S(1)}, u32[]{:S(2)}, u32[]{:S(2)}) %collective-permute-start) | collective-permute-done | bytes 524320 | tf_op jit(solution)/shard_map/ppermute | solution.py:226
  30.1 2.5 %shard_map.94 = (f32[512,512]{1,0:T(8,128)S(1)}, f32[512,512]{1,0:T(8,128)S(1)}, f32[512,512]{1,0:T(8,128)S(1)}, f32[512,512]{1,0:T(8,128)S(1)}) custom-call(f32[256,512]{1,0:T(8,128)S(1)} %shard_map.93.own_full, f32[256,512]{1,0:T(8,128)S(1)} %collective-permute-done.other_full, f32[4,256,512]{2,1,0:T(8,128)} %own_far.1, ...), custom_call_target="tpu_custom_call" | custom-call | flops 1048576 | bytes 8388608 | tf_op jit(solution)/shard_map/pallas_call | solution.py:154
  32.6 1.0 copy-done
  33.7 1.2 copy-done.1
  34.9 0.7 shard_map.95
  35.5 14.1 %all_to_all.40 = f32[16,8,512]{2,1,0:T(8,128)S(1)} all-to-all(f32[16,8,512]{2,1,0:T(8,128)S(1)} %shard_map.95), channel_id=1, replica_groups=mesh['chip'=16,'core'=2,'col'=16] {'chip'}, dimensions={0} | all-to-all | bytes 524288 | tf_op jit(solution)/shard_map/all_to_all | solution.py:198
  49.7 10.2 %all_to_all.41.known = f32[16,8,512]{2,1,0:T(8,128)S(1)} all-to-all(f32[16,8,512]{2,1,0:T(8,128)S(1)} %broadcast_in_dim.9), channel_id=1, replica_groups=mesh['chip'=16,'core'=2,'col'=16] {'chip'}, dimensions={0} | all-to-all | bytes 524288 | tf_op jit(solution)/shard_map/all_to_all | solution.py:194
  59.9 0.7 shard_map.96
  60.5 25.1 %all_to_all.42 = f32[16,8,512]{2,1,0:T(8,128)S(1)} all-to-all(f32[16,8,512]{2,1,0:T(8,128)S(1)} %shard_map.96), channel_id=1, replica_groups=mesh['chip'=16,'core'=2,'col'=16] {'col'}, dimensions={0} | all-to-all | bytes 524288 | tf_op jit(solution)/shard_map/all_to_all | solution.py:198
  85.7 22.6 %all_to_all.43.known = f32[16,8,512]{2,1,0:T(8,128)S(1)} all-to-all(f32[16,8,512]{2,1,0:T(8,128)S(1)} %broadcast_in_dim.10), channel_id=1, replica_groups=mesh['chip'=16,'core'=2,'col'=16] {'col'}, dimensions={0} | all-to-all | bytes 524288 | tf_op jit(solution)/shard_map/all_to_all | solution.py:194
  108.3 0.7 shard_map.97
  109.0 10.4 %all_to_all.44 = f32[16,8,512]{2,1,0:T(8,128)S(1)} all-to-all(f32[16,8,512]{2,1,0:T(8,128)S(1)} %shard_map.97), channel_id=1, replica_groups=mesh['chip'=16,'core'=2,'col'=16] {'chip'}, dimensions={0} | all-to-all | bytes 524288 | tf_op jit(solution)/shard_map/all_to_all | solution.py:198
  119.5 10.2 %all_to_all.45.known = f32[16,8,512]{2,1,0:T(8,128)S(1)} all-to-all(f32[16,8,512]{2,1,0:T(8,128)S(1)} %broadcast_in_dim.11), channel_id=1, replica_groups=mesh['chip'=16,'core'=2,'col'=16] {'chip'}, dimensions={0} | all-to-all | bytes 524288 | tf_op jit(solution)/shard_map/all_to_all | solution.py:194
  129.6 0.7 shard_map.98
  130.3 22.7 %all_to_all.46 = f32[16,8,512]{2,1,0:T(8,128)S(1)} all-to-all(f32[16,8,512]{2,1,0:T(8,128)S(1)} %shard_map.98), channel_id=1, replica_groups=mesh['chip'=16,'core'=2,'col'=16] {'col'}, dimensions={0} | all-to-all | bytes 524288 | tf_op jit(solution)/shard_map/all_to_all | solution.py:198
  153.0 10.0 %all-gather.1 = f32[4,8,512]{2,1,0:T(8,128)S(1)} all-gather(f32[2,8,512]{2,1,0:T(8,128)S(1)} %pad_maximum_fusion), channel_id=3, replica_groups=mesh['chip'=16,'core'=2,'col'=16] {'core'}, dimensions={0}, use_global_device_ids=true | all-gather | bytes 98304 | tf_op jit(solution)/shard_map/all_gather | solution.py:234
  163.0 0.6 fusion.2
  (22 shorter events, 0.3 us)
Async XLA Ops:
  10.1 23.6 %all-to-all-start = ((f32[16,8,512]{2,1,0:T(8,128)}), f32[16,8,512]{2,1,0:T(8,128)S(1)}, u32[]{:S(2)}, u32[]{:S(2)}) async-start(f32[16,8,512]{2,1,0:T(8,128)} %broadcast_in_dim.8), calls=%async_computation | async-start | bytes 524288 | tf_op jit(solution)/shard_map/all_to_all | solution.py:222
  19.6 10.5 %collective-permute-start.1 = (f32[4,256,512]{2,1,0:T(8,128)}, f32[4,256,512]{2,1,0:T(8,128)S(1)}, u32[]{:S(2)}, u32[]{:S(2)}) collective-permute-start(f32[4,256,512]{2,1,0:T(8,128)} %own_far.1), channel_id=1, source_target_pairs={{0,16},{16,0},{1,17},{17,1},{2,18},{18,2},{3,19},{19,3},{4,20},{20... | collective-permute-start | bytes 6291464 | tf_op jit(solution)/shard_map/ppermute | solution.py:228
  22.2 0.7 copy-start.2
  26.3 3.8 %collective-permute-start = (f32[256,512]{1,0:T(8,128)S(1)}, f32[256,512]{1,0:T(8,128)S(1)}, u32[]{:S(2)}, u32[]{:S(2)}) collective-permute-start(f32[256,512]{1,0:T(8,128)S(1)} %shard_map.93.own_full), channel_id=1, source_target_pairs={{0,16},{16,0},{1,17},{17,1},{2,18},{18,2},{3,19},{19,3},{4,20},{20... | collective-permute-start | bytes 1572872 | tf_op jit(solution)/shard_map/ppermute | solution.py:226
  32.6 1.0 copy-start
  33.6 1.2 copy-start.1
  49.7 59.3 %copy-start.3 = (f32[8,512]{1,0:T(8,128)}, f32[8,512]{1,0:T(8,128)S(1)}, u32[]{:S(2)}) copy-start(f32[8,512]{1,0:T(8,128)S(1)} %reduce_sum.36) | copy-start | bytes 49156
  119.4 44.2 %copy-start.4 = (f32[8,512]{1,0:T(8,128)}, f32[8,512]{1,0:T(8,128)S(1)}, u32[]{:S(2)}) copy-start(f32[8,512]{1,0:T(8,128)S(1)} %reduce_sum.38) | copy-start | bytes 49156

commit v4 on v3

--- a/solution.py
+++ b/solution.py
@@ -1,3 +1,5 @@
+import functools
+
 import jax
 import jax.numpy as jnp
 from jax import lax
@@ -120,50 +122,54 @@
     )(corner, coupling, sites, classes, vertex)
 
 
-def weigh_kernel(own_full, other_full, own_far, others_far, *rest):
-    loops, half = own_far.shape[:2]
-    weighted_far, (weighted, bubbles, gone, arrived) = rest[:loops], rest[loops:]
+def weigh_kernel(steps, own_full, other_full, own_far, others_far, *rest):
+    half = own_far.shape[1]
+    outs, (weighted, bubbles, gone, arrived) = rest[: len(steps)], rest[len(steps) :]
     copies = fetch(
         [
-            (far.at[step], bubbles.at[step, pl.ds(half * index, half)])
-            for step in range(loops)
+            (far.at[step], bubbles.at[place, pl.ds(half * index, half)])
+            for place, step in enumerate(steps)
             for index, far in enumerate((own_far, others_far))
         ],
         arrived,
     )
     leaving = []
-    for step in range(loops):
+    for place, step in enumerate(steps):
+        stays = len(steps) == 1
+        near = outs[0] if stays else weighted.at[place]
         for index, full in enumerate((own_full, other_full)):
-            copies[2 * step + index].wait()
+            copies[2 * place + index].wait()
             rows = pl.ds(half * index, half)
-            product = bubbles[step, rows, :] * full[...]
+            product = bubbles[place, rows, :] * full[...]
             if step % 2:
-                weighted[step, :, rows] = product.T
+                near[:, rows] = product.T
             else:
-                weighted[step, rows, :] = product
-        leaving.append(pltpu.make_async_copy(weighted.at[step], weighted_far[step], gone.at[step]))
-        leaving[-1].start()
+                near[rows, :] = product
+        if not stays:
+            leaving.append(pltpu.make_async_copy(near, outs[place], gone.at[place]))
+            leaving[-1].start()
     for copy in leaving:
         copy.wait()
 
 
-def weigh(own_full, other_full, bubbles, other_bubbles):
-    loops, half, cols = bubbles.shape
+def weigh(steps, own_full, other_full, bubbles, other_bubbles):
+    half, cols = bubbles.shape[1:]
+    count = len(steps)
     near = pl.BlockSpec(memory_space=pltpu.VMEM)
     far = pl.BlockSpec(memory_space=pl.ANY)
     return pl.pallas_call(
-        weigh_kernel,
-        out_shape=[jax.ShapeDtypeStruct((2 * half, cols), jnp.float32)] * loops,
+        functools.partial(weigh_kernel, steps),
+        out_shape=[jax.ShapeDtypeStruct((2 * half, cols), jnp.float32)] * count,
         in_specs=[near, near, far, far],
-        out_specs=[far] * loops,
+        out_specs=[near if count == 1 else far] * count,
         scratch_shapes=[
-            pltpu.VMEM((loops, 2 * half, cols), jnp.float32),
-            pltpu.VMEM((loops, 2 * half, cols), jnp.float32),
-            pltpu.SemaphoreType.DMA((loops,)),
-            pltpu.SemaphoreType.DMA((2 * loops,)),
+            pltpu.VMEM((count, 2 * half, cols), jnp.float32),
+            pltpu.VMEM((count, 2 * half, cols), jnp.float32),
+            pltpu.SemaphoreType.DMA((count,)),
+            pltpu.SemaphoreType.DMA((2 * count,)),
         ],
         cost_estimate=pl.CostEstimate(
-            flops=2 * loops * half * cols, bytes_accessed=16 * loops * half * cols, transcendentals=0
+            flops=2 * count * half * cols, bytes_accessed=16 * count * half * cols, transcendentals=0
         ),
         compiler_params=pltpu.CompilerParams(vmem_limit_bytes=24 * 1024 * 1024),
     )(own_full, other_full, pltpu.with_memory_space_constraint(bubbles, pltpu.HBM), other_bubbles)
@@ -190,6 +196,55 @@
     )(known, weighted)
 
 
+def first_kernel(core, known, weighted, out):
+    half = known.shape[2]
+    product = jnp.dot(
+        known[core[0]],
+        weighted[pl.ds(0, half), :],
+        precision=HIGHEST,
+        preferred_element_type=jnp.float32,
+    ) + jnp.dot(
+        known[1 - core[0]],
+        weighted[pl.ds(half, half), :],
+        precision=HIGHEST,
+        preferred_element_type=jnp.float32,
+    )
+    out[...] = product.reshape(out.shape)
+
+
+def first_product(core, known, weighted):
+    near = pl.BlockSpec(memory_space=pltpu.VMEM)
+    parts, slab, half = known.shape
+    return pl.pallas_call(
+        first_kernel,
+        out_shape=jax.ShapeDtypeStruct((parts // 2, slab, 2 * half), jnp.float32),
+        in_specs=[pl.BlockSpec(memory_space=pltpu.SMEM), near, near],
+        out_specs=near,
+        compiler_params=pltpu.CompilerParams(vmem_limit_bytes=16 * 1024 * 1024),
+    )(core, known.reshape(2, -1, half), weighted)
+
+
+def settle_kernel(core, both, *terms):
+    slab, half = both.shape[2], both.shape[3] // 2
+    leads = jnp.broadcast_to(core[0], (slab, half)) == 0
+    for step, term in enumerate(terms):
+        for index in range(2):
+            front, back = both[index, step, :, :half], both[index, step, :, half:]
+            chosen = jnp.where(leads, back, front) if index else jnp.where(leads, front, back)
+            term[pl.ds(slab * index, slab), :] = chosen
+
+
+def settle(core, both):
+    cores, count, slab, rows = both.shape
+    near = pl.BlockSpec(memory_space=pltpu.VMEM)
+    return pl.pallas_call(
+        settle_kernel,
+        out_shape=[jax.ShapeDtypeStruct((cores * slab, rows // 2), jnp.float32)] * count,
+        in_specs=[pl.BlockSpec(memory_space=pltpu.SMEM), near],
+        out_specs=[near] * count,
+    )(core, both)
+
+
 def gather(piece, axis, parts):
     return lax.all_to_all(jnp.broadcast_to(piece[None], (parts, *piece.shape)), axis, 0, 0)
 
@@ -203,39 +258,35 @@
 
     def per_device(vertex, bubbles, site_panel, bond_sites, bond_class, coupling):
         half, cols_blk = vertex.shape
-        core = lax.axis_index("core")
+        core = lax.axis_index("core").astype(jnp.int32).reshape(1)
         corner = jnp.stack(
             [lax.axis_index(("chip", "core")) * half, lax.axis_index("col") * cols_blk]
         ).astype(jnp.int32)
         groups = bond_class.shape[0] // LANES
         sites = bond_sites.reshape(groups, LANES, 2).transpose(0, 2, 1).reshape(2 * groups, LANES)
-        panels = lax.all_gather(site_panel.T, "core")
-        wide = panels.reshape(2, 2, panels.shape[1] // 2, half)
-        held = jnp.where(core == 0, wide[:, 0], wide[:, 1])
-        current = jnp.where(
-            core == 0,
-            jnp.concatenate([held[0], held[1]], axis=1),
-            jnp.concatenate([held[1], held[0]], axis=1),
-        )
-        sent = jnp.broadcast_to(current[None], (cols_n, *current.shape))
+        slab = site_panel.shape[1] // 2
+        sent = jnp.broadcast_to(
+            site_panel.T.reshape(2, 1, slab, half), (2, cols_n, slab, half)
+        ).reshape(2 * cols_n, slab, half)
         sent, corner, sent_bubbles = lax.optimization_barrier((sent, corner, bubbles))
-        known = lax.all_to_all(sent, "col", 0, 0)
+        known = lax.all_to_all(sent, ("core", "col"), 0, 0)
         full = place(vertex, sites, bond_class.reshape(groups, LANES), coupling, corner)
-        weighted = weigh(
+        blocks = (
             full,
             lax.ppermute(full, "core", swap),
             bubbles,
             lax.ppermute(sent_bubbles, "core", swap),
         )
-        first = scatter_sum(product(known, weighted[0]), "chip")
+        later = weigh(tuple(range(1, bubbles.shape[0])), *blocks)
+        own_full, later = lax.optimization_barrier((blocks[0], later))
+        weighted = weigh((0,), own_full, *blocks[1:]) + tuple(later)
+        first = scatter_sum(first_product(core, known, weighted[0]), "chip")
         second = scatter_sum(product(gather(first, "chip", chips), weighted[1]), "col")
         third = scatter_sum(product(gather(second, "col", cols_n), weighted[2]), "chip")
         fourth = scatter_sum(product(gather(third, "chip", chips), weighted[3]), "col")
         both = lax.all_gather(jnp.stack([second, fourth]), "core")
-        swapped = jnp.where(core == 0, both[0, :, :, :half], both[0, :, :, half:])
-        straight = jnp.where(core == 0, both[1, :, :, half:], both[1, :, :, :half])
-        even_terms = jnp.concatenate([swapped, straight], axis=1)
-        return first.T, even_terms[0].T, third.T, even_terms[1].T
+        second, fourth = settle(core, both)
+        return first.T, second.T, third.T, fourth.T
 
     return per_device
 

time: 164 us -> 164 us (level)
  blocking collectives: 134 us -> 118 us
  starting transfers between devices: 14 us -> 21.1 us
  waiting for transfers between devices: 1.96 us -> 8.74 us
  Pallas kernels: 8.56 us -> 11 us
    all_gather x1 -> x0, blocking collectives: 8.58 us -> none  [per_device(): panels = lax.all_gather(site_panel.T, 'core')]
    all_to_all x4, blocking collectives: 72.3 us -> 64.8 us  [scatter_sum(): return jnp.sum(lax.all_to_all(pieces, axis, 0, 0), axis=0)]
    all_to_all x1, starting transfers between devices: 9.54 us -> 16.8 us  [per_device(): known = lax.all_to_all(sent, ('core', 'col'), 0, 0)]
    all_to_all x1, waiting for transfers between devices: 0.08 us -> 7.13 us  [per_device(): known = lax.all_to_all(sent, ('core', 'col'), 0, 0)]
    pallas_call x1 -> x4, Pallas kernels: 2.5 us -> 5.57 us  [the longest x2 3.46 us: weigh(): pl.pallas_call(functools.partial(weigh_kernel, steps), out_shape=[jax.Sha...]
where the time goes in v4:
time: 164 us; the launch traced here: 163 us
  blocking collectives  118 us (72%)
  starting transfers between devices  21.1 us (13%)
  Pallas kernels  11 us (7%)
  waiting for transfers between devices  8.74 us (5%)
  local copies, waits for them, and re-layouts  3.16 us (2%)
    all_to_all x4, blocking collectives, scatter_sum(): return jnp.sum(lax.all_to_all(pieces, axis, 0, 0), axis=0)  64.8 us
    all_to_all x3, blocking collectives, gather(): lax.all_to_all(jnp.broadcast_to(piece[None], (parts, *piece.shape)), axis...  43.5 us
    all_to_all x1, starting transfers between devices, per_device(): known = lax.all_to_all(sent, ('core', 'col'), 0, 0)  16.8 us
    all_gather x1, blocking collectives, per_device(): both = lax.all_gather(jnp.stack([second, fourth]), 'core')  10.2 us
    all_to_all x1, waiting for transfers between devices, per_device(): known = lax.all_to_all(sent, ('core', 'col'), 0, 0)  7.13 us
    pallas_call x2, Pallas kernels, weigh(): pl.pallas_call(functools.partial(weigh_kernel, steps), out_shape=[jax.Sha...  3.46 us
    pallas_call x1, Pallas kernels, place(): pl.pallas_call(place_kernel, out_shape=pltpu.VMEM(vertex.shape, jnp.float...  3.45 us
  transfers between devices with their start and end apart: 3, of which 2 were waited for; matrix products, arithmetic and copies ran while one was open for 0% of the time, Pallas kernels for 4%

profile of v4, /device:TPU:1, one launch (start us, length us, event | category | flops | bytes accessed | tf_op | source)
XLA Modules:
  0.0 163.3 jit_solution(7585158062025051884)
XLA Ops:
  0.7 1.5 broadcast_in_dim.11
  2.2 16.8 %all-to-all-start = ((f32[32,8,256]{2,1,0:T(8,128)}), f32[32,8,256]{2,1,0:T(8,128)S(1)}, u32[]{:S(2)}, u32[]{:S(2)}) async-start(f32[32,8,256]{2,1,0:T(8,128)} %bitcast.3), calls=%async_computation | async-start | bytes 524288 | tf_op jit(solution)/shard_map/all_to_all | solution.py:272
  18.9 2.1 %collective-permute-start.1 = (f32[4,256,512]{2,1,0:T(8,128)}, f32[4,256,512]{2,1,0:T(8,128)S(1)}, u32[]{:S(2)}, u32[]{:S(2)}) collective-permute-start(f32[4,256,512]{2,1,0:T(8,128)} %own_far.3), channel_id=1, source_target_pairs={{0,16},{16,0},{1,17},{17,1},{2,18},{18,2},{3,19},{19,3},{4,20},{20... | collective-permute-start | bytes 6291464 | tf_op jit(solution)/shard_map/ppermute | solution.py:278
  21.1 0.6 copy-done.2
  21.7 3.4 %shard_map.93.own_full = f32[256,512]{1,0:T(8,128)S(1)} custom-call(s32[2]{0:T(128)S(1)} %pad_add_fusion.corner, f32[16]{0:T(128)S(1)} %copy-done.2, s32[384,128]{1,0:T(8,128)} %bitcast.28, s32[192,128]{1,0:T(8,128)} %bitcast.29, f32[256,512]{1,0:T(8,128)} %vertex_far.1), custom_call_target="tpu_custom_call" | custom-call | flops 20000000000 | bytes 1000000 | tf_op jit(solution)/shard_map/pallas_call | solution.py:107
  25.2 2.2 %collective-permute-start = (f32[256,512]{1,0:T(8,128)S(1)}, f32[256,512]{1,0:T(8,128)S(1)}, u32[]{:S(2)}, u32[]{:S(2)}) collective-permute-start(f32[256,512]{1,0:T(8,128)S(1)} %shard_map.93.own_full), channel_id=1, source_target_pairs={{0,16},{16,0},{1,17},{17,1},{2,18},{18,2},{3,19},{19,3},{4,20},{20... | collective-permute-start | bytes 1572872 | tf_op jit(solution)/shard_map/ppermute | solution.py:276
  27.4 1.6 collective-permute-done.other_full
  29.0 2.3 %shard_map.94 = (f32[512,512]{1,0:T(8,128)S(1)}, f32[512,512]{1,0:T(8,128)S(1)}, f32[512,512]{1,0:T(8,128)S(1)}) custom-call(f32[256,512]{1,0:T(8,128)S(1)} %shard_map.93.own_full, f32[256,512]{1,0:T(8,128)S(1)} %collective-permute-done.other_full, f32[4,256,512]{2,1,0:T(8,128)} %own_far.3, f32[4,256,512]{2,1,0:T(8,128)S(1)} %collective-permute-done.1.others_far), custom_call_target="tpu_custom_call" | custom-call | flops 786432 | bytes 6291456 | tf_op jit(solution)/shard_map/pallas_call | solution.py:160
  31.3 1.0 copy-done
  32.3 1.2 shard_map.95.weighted
  33.5 7.1 %all-to-all-done = f32[32,8,256]{2,1,0:T(8,128)S(1)} async-done(((f32[32,8,256]{2,1,0:T(8,128)}), f32[32,8,256]{2,1,0:T(8,128)S(1)}, u32[]{:S(2)}, u32[]{:S(2)}) %all-to-all-start) | async-done | bytes 262176 | tf_op jit(solution)/shard_map/all_to_all | solution.py:272
  40.6 0.7 shard_map.96
  41.3 15.3 %all_to_all.40 = f32[16,8,512]{2,1,0:T(8,128)S(1)} all-to-all(f32[16,8,512]{2,1,0:T(8,128)S(1)} %shard_map.96), channel_id=1, replica_groups=mesh['chip'=16,'core'=2,'col'=16] {'chip'}, dimensions={0} | all-to-all | bytes 524288 | tf_op jit(solution)/shard_map/all_to_all | solution.py:253
  56.7 10.7 %all_to_all.41.known = f32[16,8,512]{2,1,0:T(8,128)S(1)} all-to-all(f32[16,8,512]{2,1,0:T(8,128)S(1)} %broadcast_in_dim.12), channel_id=1, replica_groups=mesh['chip'=16,'core'=2,'col'=16] {'chip'}, dimensions={0} | all-to-all | bytes 524288 | tf_op jit(solution)/shard_map/all_to_all | solution.py:249
  67.4 0.7 shard_map.97
  68.0 16.3 %all_to_all.42 = f32[16,8,512]{2,1,0:T(8,128)S(1)} all-to-all(f32[16,8,512]{2,1,0:T(8,128)S(1)} %shard_map.97), channel_id=1, replica_groups=mesh['chip'=16,'core'=2,'col'=16] {'col'}, dimensions={0} | all-to-all | bytes 524288 | tf_op jit(solution)/shard_map/all_to_all | solution.py:253
  84.4 22.6 %all_to_all.43.known = f32[16,8,512]{2,1,0:T(8,128)S(1)} all-to-all(f32[16,8,512]{2,1,0:T(8,128)S(1)} %broadcast_in_dim.13), channel_id=1, replica_groups=mesh['chip'=16,'core'=2,'col'=16] {'col'}, dimensions={0} | all-to-all | bytes 524288 | tf_op jit(solution)/shard_map/all_to_all | solution.py:249
  107.0 0.7 shard_map.98
  107.7 10.4 %all_to_all.44 = f32[16,8,512]{2,1,0:T(8,128)S(1)} all-to-all(f32[16,8,512]{2,1,0:T(8,128)S(1)} %shard_map.98), channel_id=1, replica_groups=mesh['chip'=16,'core'=2,'col'=16] {'chip'}, dimensions={0} | all-to-all | bytes 524288 | tf_op jit(solution)/shard_map/all_to_all | solution.py:253
  118.2 10.2 %all_to_all.45.known = f32[16,8,512]{2,1,0:T(8,128)S(1)} all-to-all(f32[16,8,512]{2,1,0:T(8,128)S(1)} %broadcast_in_dim.14), channel_id=1, replica_groups=mesh['chip'=16,'core'=2,'col'=16] {'chip'}, dimensions={0} | all-to-all | bytes 524288 | tf_op jit(solution)/shard_map/all_to_all | solution.py:249
  128.3 0.7 shard_map.99
  129.0 22.7 %all_to_all.46 = f32[16,8,512]{2,1,0:T(8,128)S(1)} all-to-all(f32[16,8,512]{2,1,0:T(8,128)S(1)} %shard_map.99), channel_id=1, replica_groups=mesh['chip'=16,'core'=2,'col'=16] {'col'}, dimensions={0} | all-to-all | bytes 524288 | tf_op jit(solution)/shard_map/all_to_all | solution.py:253
  151.7 10.2 %all-gather = f32[4,8,512]{2,1,0:T(8,128)} all-gather(f32[2,8,512]{2,1,0:T(8,128)S(1)} %pad_maximum_fusion), channel_id=2, replica_groups=mesh['chip'=16,'core'=2,'col'=16] {'core'}, dimensions={0}, use_global_device_ids=true | all-gather | bytes 98304 | tf_op jit(solution)/shard_map/all_gather | solution.py:287
  161.9 1.5 shard_map.100
  (18 shorter events, 0.2 us)
Async XLA Ops:
  2.2 38.4 %all-to-all-start = ((f32[32,8,256]{2,1,0:T(8,128)}), f32[32,8,256]{2,1,0:T(8,128)S(1)}, u32[]{:S(2)}, u32[]{:S(2)}) async-start(f32[32,8,256]{2,1,0:T(8,128)} %bitcast.3), calls=%async_computation | async-start | bytes 524288 | tf_op jit(solution)/shard_map/all_to_all | solution.py:272
  18.9 10.1 %collective-permute-start.1 = (f32[4,256,512]{2,1,0:T(8,128)}, f32[4,256,512]{2,1,0:T(8,128)S(1)}, u32[]{:S(2)}, u32[]{:S(2)}) collective-permute-start(f32[4,256,512]{2,1,0:T(8,128)} %own_far.3), channel_id=1, source_target_pairs={{0,16},{16,0},{1,17},{17,1},{2,18},{18,2},{3,19},{19,3},{4,20},{20... | collective-permute-start | bytes 6291464 | tf_op jit(solution)/shard_map/ppermute | solution.py:278
  21.1 0.7 copy-start.2
  25.2 3.8 %collective-permute-start = (f32[256,512]{1,0:T(8,128)S(1)}, f32[256,512]{1,0:T(8,128)S(1)}, u32[]{:S(2)}, u32[]{:S(2)}) collective-permute-start(f32[256,512]{1,0:T(8,128)S(1)} %shard_map.93.own_full), channel_id=1, source_target_pairs={{0,16},{16,0},{1,17},{17,1},{2,18},{18,2},{3,19},{19,3},{4,20},{20... | collective-permute-start | bytes 1572872 | tf_op jit(solution)/shard_map/ppermute | solution.py:276
  31.3 1.0 copy-start
  41.3 26.1 %copy-start.1 = (f32[512,512]{1,0:T(8,128)S(1)}, f32[512,512]{1,0:T(8,128)}, u32[]{:S(2)}) copy-start(f32[512,512]{1,0:T(8,128)} %copy-done) | copy-start | bytes 3145732
  56.6 51.0 %copy-start.3 = (f32[8,512]{1,0:T(8,128)}, f32[8,512]{1,0:T(8,128)S(1)}, u32[]{:S(2)}) copy-start(f32[8,512]{1,0:T(8,128)S(1)} %reduce_sum.36) | copy-start | bytes 49156
  118.1 45.2 %copy-start.4 = (f32[8,512]{1,0:T(8,128)}, f32[8,512]{1,0:T(8,128)S(1)}, u32[]{:S(2)}) copy-start(f32[8,512]{1,0:T(8,128)S(1)} %reduce_sum.38) | copy-start | bytes 49156
